TPU v7x, 32 devices: a whole 2x2x4 slice. The times are simulated.
32 devices in a mesh: groups: 2 (over x), atoms: 16 (over z, y, core).
Axes of the slice: x: 2, y: 2, z: 4, core: 2. Of those that a mesh axis runs over, the one named last changes fastest.
Arguments:
- node_feat: bfloat16 [2048, 128], P(('groups', 'atoms')), parts along dimension 0, may hold values from -6 to 6
- species: int32 [2048], P(('groups', 'atoms')), parts along dimension 0, may hold values from 0 to 1
- positions: float32 [2048, 3], P(('groups', 'atoms')), parts along dimension 0, may hold values from 0 to 12
- pair_second: int32 [65536], P(('groups', 'atoms')), parts along dimension 0, may hold values from 0 to 127
- pair_mask: int32 [65536], P(('groups', 'atoms')), parts along dimension 0, may hold values 0 or 1
- x_vec: bfloat16 [26624, 512], P(('groups', 'atoms')), parts along dimension 0, may hold values from -6 to 6
- species_table: bfloat16 [2, 128], replicated, may hold values from -4 to 4
- onsite_table: float32 [2, 13], replicated, may hold values from -1 to 1
- w_first: bfloat16 [128, 256], replicated, may hold values from -0.375 to 0.375
- w_second: bfloat16 [128, 256], replicated, may hold values from -0.375 to 0.375
- w_radial: bfloat16 [32, 256], replicated, may hold values from -1 to 1
- w_out: bfloat16 [256, 169], replicated, may hold values from -0.375 to 0.375
Outputs:
- first_step: bfloat16 [26624, 512], P(('groups', 'atoms')), parts along dimension 0
- filtered: float32 [26624, 512], P(('groups', 'atoms')), parts along dimension 0
There are 2 independent parts, one for each index of `groups`. A program takes and returns all parts, laid end to end along the dimension named above; an argument that names none is the same for every part. Nothing has to cross between parts.
All inputs are finite; a program needn't handle non-finite values. No bound on the sum of `pair_mask` on one device may be relied on, other than what follows from the above.
Results may differ from a plain program's by a relative error of at most 0.0058.
Values may be sent and summed in bfloat16 or wider, within the bound.
A program may use at most 128 MiB of HBM per device.

v0:
```python
import jax
import jax.numpy as jnp
from jax import lax
from jax.sharding import PartitionSpec as P

ORB = 13
NRBF = 32
SPECIES = 2
NEIGH = 32


def passed_along(value, axis, steps):
    count = lax.axis_size(axis)
    pairs = [(source, (source + steps) % count) for source in range(count)]
    return lax.ppermute(value, axis, pairs)


def pair_blocks(
    feat, window_feat, positions, window_pos, second, mask, w_first, w_second, w_radial, w_out
):
    count = feat.shape[0]
    width = window_feat.shape[0]
    partner = second.reshape(count, NEIGH)
    picker = (partner[:, :, None] == jnp.arange(width, dtype=jnp.int32)[None, None, :]).reshape(
        count * NEIGH, width
    )
    partner_pos = jnp.dot(picker.astype(jnp.float32), window_pos, precision=lax.Precision.HIGHEST)
    diff = positions[:, None, :] - partner_pos.reshape(count, NEIGH, 3)
    dist_sq = jnp.sum(diff * diff, axis=-1).reshape(count * NEIGH)
    centres = jnp.arange(NRBF, dtype=jnp.float32) * (2.0 / (NRBF - 1))
    radial = jnp.exp(-(((dist_sq[:, None] / 64.0 - centres[None, :]) * 8.0) ** 2)).astype(
        jnp.bfloat16
    )
    partner_feat = jnp.dot(
        picker.astype(jnp.bfloat16), window_feat, preferred_element_type=jnp.float32
    ).astype(jnp.bfloat16)
    own_term = jnp.dot(feat, w_first, preferred_element_type=jnp.float32)
    pre = own_term[:, None, :] + jnp.dot(
        partner_feat, w_second, preferred_element_type=jnp.float32
    ).reshape(count, NEIGH, -1)
    pre = pre + jnp.dot(radial, w_radial, preferred_element_type=jnp.float32).reshape(
        count, NEIGH, -1
    )
    hidden = jax.nn.silu(pre).astype(jnp.bfloat16).reshape(count * NEIGH, -1)
    factor = mask.astype(jnp.float32) / jnp.sqrt(jnp.float32(2 * ORB * NEIGH))
    blocks = jnp.dot(hidden, w_out, preferred_element_type=jnp.float32) * factor[:, None]
    return (blocks.reshape(count, NEIGH, ORB * ORB), partner)


def place_tiles(blocks, partner, width):
    count = blocks.shape[0]
    select = (partner[:, :, None] == jnp.arange(width, dtype=jnp.int32)[None, None, :]).astype(
        jnp.float32
    )
    placed = lax.dot_general(
        select, blocks, (((1,), (1,)), ((0,), (0,))), precision=lax.Precision.HIGHEST
    )
    return placed.reshape(count, width, ORB, ORB)


def as_matrix(tiles):
    rows_n, cols_n = (tiles.shape[0], tiles.shape[1])
    return tiles.transpose(0, 2, 1, 3).reshape(rows_n * ORB, cols_n * ORB).astype(jnp.bfloat16)


def on_device(
    node_feat,
    species,
    positions,
    pair_second,
    pair_mask,
    x_vec,
    species_table,
    onsite_table,
    w_first,
    w_second,
    w_radial,
    w_out,
):
    count = node_feat.shape[0]
    onehot = (species[:, None] == jnp.arange(SPECIES, dtype=jnp.int32)[None, :]).astype(
        jnp.bfloat16
    )
    feat = (
        node_feat.astype(jnp.float32)
        + jnp.dot(onehot, species_table, preferred_element_type=jnp.float32)
    ).astype(jnp.bfloat16)
    onsite = jnp.dot(
        onehot.astype(jnp.float32), onsite_table, precision=lax.Precision.HIGHEST
    ).reshape(count * ORB)
    next_feat, next_pos = passed_along((feat.astype(jnp.float32), positions), "atoms", -1)
    window_feat = jnp.concatenate([feat, next_feat.astype(jnp.bfloat16)], axis=0)
    window_pos = jnp.concatenate([positions, next_pos], axis=0)
    blocks, partner = pair_blocks(
        feat,
        window_feat,
        positions,
        window_pos,
        pair_second,
        pair_mask,
        w_first,
        w_second,
        w_radial,
        w_out,
    )
    tiles = place_tiles(blocks, partner, 2 * count)
    own_tiles = tiles[:, :count]
    square = as_matrix(own_tiles + own_tiles.transpose(1, 0, 3, 2))
    upper = as_matrix(tiles[:, count:])
    contract_rows = (((0,), (0,)), ((), ()))
    lower_blocks = passed_along(upper, "atoms", 1)

    def apply(vec):
        sides = [passed_along(vec, "atoms", by) for by in (-1, 1)]
        result = jnp.dot(square, vec, preferred_element_type=jnp.float32)
        result = result + jnp.dot(upper, sides[0], preferred_element_type=jnp.float32)
        result = result + lax.dot_general(
            lower_blocks, sides[1], contract_rows, preferred_element_type=jnp.float32
        )
        return result + onsite[:, None] * vec.astype(jnp.float32)

    first_step = apply(x_vec).astype(jnp.bfloat16)
    filtered = 2.0 * apply(first_step) - x_vec.astype(jnp.float32)
    return (first_step, filtered)


def solution(mesh):
    return jax.shard_map(
        on_device,
        mesh=mesh,
        in_specs=(
            P(("groups", "atoms"), None),
            P(("groups", "atoms")),
            P(("groups", "atoms"), None),
            P(("groups", "atoms")),
            P(("groups", "atoms")),
            P(("groups", "atoms"), None),
            P(),
            P(),
            P(),
            P(),
            P(),
            P(),
        ),
        out_specs=(P(("groups", "atoms"), None), P(("groups", "atoms"), None)),
        check_vma=False,
    )
```

profile of v0, /device:TPU:1, one launch (start us, length us, event | category | flops | bytes accessed | tf_op | source)
XLA Modules:
  0.0 151.7 jit_solution(1629851617071425180)
XLA Ops:
  0.6 0.0 copy-start
  0.6 0.1 collective-permute-start.2
  0.8 2.6 %collective-permute-start.4 = (bf16[832,512]{1,0:T(8,128)(2,1)}, bf16[832,512]{1,0:T(8,128)(2,1)}, u32[]{:S(2)}, u32[]{:S(2)}) collective-permute-start(bf16[832,512]{1,0:T(8,128)(2,1)} %param.17), channel_id=1, source_target_pairs={{0,1},{1,2},{2,3},{3,4},{4,5},{5,6},{6,7},{7,8},{8,9},{9,10},{10,1... | collective-permute-start | bytes 2555912 | tf_op jit(solution)/shard_map/ppermute | solution.py:15
  3.4 2.8 %collective-permute-start.1 = (f32[64,3]{0,1:T(4,128)}, f32[64,3]{0,1:T(4,128)S(1)}, u32[]{:S(2)}, u32[]{:S(2)}) collective-permute-start(f32[64,3]{0,1:T(4,128)} %param.14), channel_id=1, source_target_pairs={{0,15},{1,0},{2,1},{3,2},{4,3},{5,4},{6,5},{7,6},{8,7},{9,8},{10,9... | collective-permute-start | bytes 2312 | tf_op jit(solution)/shard_map/ppermute | solution.py:15
  6.2 0.9 fusion.7
  7.2 4.5 %collective-permute-start = (bf16[64,128]{1,0:T(8,128)(2,1)S(1)}, bf16[64,128]{1,0:T(8,128)(2,1)S(1)}, u32[]{:S(2)}, u32[]{:S(2)}) collective-permute-start(bf16[64,128]{1,0:T(8,128)(2,1)S(1)} %fusion.7), channel_id=1, source_target_pairs={{0,15},{1,0},{2,1},{3,2},{4,3},{5,4},{6,5},{7,6},{8,7},{9,8},{10,9... | collective-permute-start | bytes 49160 | tf_op jit(solution)/shard_map/ppermute | solution.py:15
  11.6 0.7 convert_multiply_fusion.1
  12.3 1.0 fusion.37
  13.3 0.0 copy-start.6
  13.3 0.8 copy.24
  14.1 0.8 eq.43
  14.9 8.2 %collective-permute-done.1 = f32[64,3]{0,1:T(4,128)S(1)} collective-permute-done((f32[64,3]{0,1:T(4,128)}, f32[64,3]{0,1:T(4,128)S(1)}, u32[]{:S(2)}, u32[]{:S(2)}) %collective-permute-start.1) | collective-permute-done | bytes 800 | tf_op jit(solution)/shard_map/ppermute | solution.py:15
  23.2 3.1 %fusion.6 = f32[64,32]{1,0:T(8,128)S(1)} fusion(s32[64,32]{1,0:T(8,128)S(1)} %eq.43, f32[64,3]{1,0:T(8,128)S(1)} %copy.24, f32[64,3]{0,1:T(4,128)S(1)} %collective-permute-done.1, f32[64,3]{0,1:T(4,128)} %param.14), kind=kOutput, calls=%fused_computation.16 | convolution fusion | flops 9716096 | bytes 18688 | tf_op jit(solution)/shard_map/dot_general | solution.py:27
  26.3 0.1 div.21
  26.4 0.0 collective-permute-done
  26.4 0.2 add.45
  26.6 0.0 copy-start.7
  26.6 2.1 %convolution_add_fusion.1 = f32[2048,256]{1,0:T(8,128)} fusion(f32[2048,256]{1,0:T(8,128)S(1)} %bitcast.44, bf16[128,256]{1,0:T(8,128)(2,1)S(1)} %copy-done.5, s32[2048]{0:T(1024)S(1)} %copy-done.6, bf16[64,128]{1,0:T(8,128)(2,1)S(1)} %collective-permute-done, bf16[64,128]{1,0:T(8,128)(2,1)S(1)} %fusion.7), kind=kOutput, calls=%fused_computation.6 | convolution fusion | flops 202440704 | bytes 4300800 | tf_op jit(solution)/shard_map/dot_general | solution.py:38
  28.7 3.7 %convolution_multiply_fusion = f32[2048,169]{0,1:T(8,128)} fusion(bf16[256,169]{0,1:T(8,128)(2,1)S(1)} %copy-done, f32[2048,256]{1,0:T(8,128)} %convolution_add_fusion.1, bf16[32,256]{1,0:T(8,128)(2,1)S(1)} %copy-done.7, f32[2048]{0:T(1024)S(1)} %convert_multiply_fusion.1, f32[32]{0:T(128)S(1)} %iota_multiply_fusion, f32[2048]{0:T(1024)S(1)} %div.21), kind=kOutput, calls=%fused_computation.7 | convolution fusion | flops 214583296 | bytes 3601024 | tf_op jit(solution)/shard_map/dot_general | solution.py:46
  32.4 1.8 %copy.25 = f32[2048,169]{1,0:T(8,128)S(1)} copy(f32[2048,169]{0,1:T(8,128)} %convolution_multiply_fusion) | data formatting | bytes 2768896 | tf_op jit(solution)/shard_map/mul | solution.py:46
  34.2 5.2 %fusion.9 = f32[64,128,169]{1,2,0:T(8,128)S(1)} fusion(f32[64,32,169]{2,1,0:T(8,128)S(1)} %bitcast.45, s32[64,32]{1,0:T(8,128)S(1)} %eq.43), kind=kOutput, calls=%fused_computation.22 | convolution fusion | flops 531890176 | bytes 6930432 | tf_op jit(solution)/shard_map/dot_general | solution.py:55
  39.4 1.8 %copy.26 = f32[64,128,169]{1,0,2:T(8,128)S(1)} copy(f32[64,128,169]{1,2,0:T(8,128)S(1)} %fusion.9) | data formatting | bytes 11075584 | tf_op jit(solution)/shard_map/dot_general | solution.py:55
  41.2 2.4 %copy-done.2 = f32[64,128,169]{1,0,2:T(8,128)} copy-done((f32[64,128,169]{1,0,2:T(8,128)}, f32[64,128,169]{1,0,2:T(8,128)S(1)}, u32[]{:S(2)}) %copy-start.2) | copy-done | bytes 5537816
  43.6 0.9 fusion.2
  44.5 10.6 %copy.29 = bf16[64,13,64,13]{3,2,1,0:T(8,128)(2,1)} copy(bf16[64,13,64,13]{2,0,3,1:T(8,128)(2,1)S(1)} %fusion.2) | data formatting | bytes 2768896 | tf_op jit(solution)/shard_map/convert_element_type | solution.py:63
  55.1 19.7 %convert_element_type.68 = bf16[832,832]{1,0:T(8,128)(2,1)} reshape(bf16[64,13,64,13]{3,2,1,0:T(8,128)(2,1)} %copy.29) | data formatting | bytes 2768896 | tf_op jit(solution)/shard_map/convert_element_type | solution.py:63
  74.8 0.0 collective-permute-start.3
  74.8 0.2 fusion.26
  75.0 0.1 mul.62
  75.2 6.9 %copy.27 = f32[64,64,13,13]{0,1,2,3:T(8,128)} copy(f32[64,64,13,13]{1,0,3,2:T(8,128)} %bitcast.42) | data formatting | bytes 5537792 | tf_op jit(solution)/shard_map/slice | solution.py:107
  82.1 5.6 %fusion.1 = bf16[64,13,64,13]{2,0,3,1:T(8,128)(2,1)S(1)} fusion(f32[64,64,13,13]{0,1,2,3:T(8,128)} %copy.27, f32[64,128,13,13]{1,0,3,2:T(8,128)} %bitcast.43), kind=kLoop, calls=%fused_computation.3 | loop fusion | flops 1384448 | bytes 6922240 | tf_op jit(solution)/shard_map/convert_element_type | solution.py:63
  87.7 10.6 %copy.28 = bf16[64,13,64,13]{3,2,1,0:T(8,128)(2,1)} copy(bf16[64,13,64,13]{2,0,3,1:T(8,128)(2,1)S(1)} %fusion.1) | data formatting | bytes 2768896 | tf_op jit(solution)/shard_map/convert_element_type | solution.py:63
  98.3 19.1 %convert_element_type.66 = bf16[832,832]{1,0:T(8,128)(2,1)S(1)} reshape(bf16[64,13,64,13]{3,2,1,0:T(8,128)(2,1)} %copy.28) | data formatting | bytes 2768896 | tf_op jit(solution)/shard_map/convert_element_type | solution.py:63
  117.4 1.0 fusion.38
  118.4 0.0 collective-permute-done.2
  118.5 2.6 %fusion.39 = f32[832,512]{1,0:T(8,128)S(1)} fusion(bf16[832,832]{1,0:T(8,128)(2,1)} %convert_element_type.68, bf16[832,512]{1,0:T(8,128)(2,1)} %collective-permute-done.2), kind=kOutput, calls=%fused_computation.49 | convolution fusion | flops 708837376 | bytes 3940352 | tf_op jit(solution)/shard_map/dot_general | solution.py:116
  121.1 0.0 collective-permute-done.4
  121.1 0.0 collective-permute-done.3
  121.1 2.8 %fusion.4 = bf16[832,512]{1,0:T(8,128)(2,1)S(1)} fusion(bf16[832,512]{1,0:T(8,128)(2,1)S(1)} %copy-done.3, f32[832,512]{1,0:T(8,128)S(1)} %fusion.38, f32[832,512]{1,0:T(8,128)S(1)} %fusion.39, bf16[832,832]{1,0:T(8,128)(2,1)} %collective-permute-done.3, bf16[832,512]{1,0:T(8,128)(2,1)} %collective-permute-done.4, f32[832]{0:T(1024)S(1)} %mul.62), kind=kOutput, calls=%fused_computation.13 | convolution fusion | flops 711393280 | bytes 7351552 | tf_op jit(solution)/shard_map/dot_general | solution.py:117
  124.0 0.0 copy-start.4
  124.0 0.6 collective-permute-start.5
  124.5 1.2 collective-permute-start.6
  125.8 1.0 fusion.40
  126.8 18.5 %collective-permute-done.5 = bf16[832,512]{1,0:T(8,128)(2,1)S(1)} collective-permute-done((bf16[832,512]{1,0:T(8,128)(2,1)S(1)}, bf16[832,512]{1,0:T(8,128)(2,1)S(1)}, u32[]{:S(2)}, u32[]{:S(2)}) %collective-permute-start.5) | collective-permute-done | bytes 852000 | tf_op jit(solution)/shard_map/ppermute | solution.py:15
  145.3 2.4 %fusion.41 = f32[832,512]{1,0:T(8,128)S(1)} fusion(bf16[832,832]{1,0:T(8,128)(2,1)} %convert_element_type.68, bf16[832,512]{1,0:T(8,128)(2,1)S(1)} %collective-permute-done.5), kind=kOutput, calls=%fused_computation.51 | convolution fusion | flops 708837376 | bytes 3940352 | tf_op jit(solution)/shard_map/dot_general | solution.py:116
  147.7 0.0 collective-permute-done.6
  147.7 0.0 copy-start.1
  147.7 3.9 %convert_subtract_fusion = f32[832,512]{1,0:T(8,128)} fusion(bf16[832,512]{1,0:T(8,128)(2,1)S(1)} %copy-done.3, bf16[832,512]{1,0:T(8,128)(2,1)S(1)} %fusion.4, f32[832,512]{1,0:T(8,128)S(1)} %fusion.40, f32[832,512]{1,0:T(8,128)S(1)} %fusion.41, bf16[832,832]{1,0:T(8,128)(2,1)} %collective-permute-done.3, bf16[832,512]{1,0:T(8,128)(2,1)S(1)} %collective-permute-done.6, ...), kind=kOutput, calls=%fused_computation.9 | convolution fusion | flops 712245248 | bytes 9055488 | tf_op jit(solution)/shard_map/dot_general | solution.py:117
  (16 shorter events, 0.0 us)
Async XLA Ops:
  0.6 28.1 %copy-start = (bf16[256,169]{0,1:T(8,128)(2,1)S(1)}, bf16[256,169]{0,1:T(8,128)(2,1)}, u32[]{:S(2)}) copy-start(bf16[256,169]{0,1:T(8,128)(2,1)} %param.23) | copy-start | bytes 259588
  0.6 117.8 %collective-permute-start.2 = (bf16[832,512]{1,0:T(8,128)(2,1)}, bf16[832,512]{1,0:T(8,128)(2,1)}, u32[]{:S(2)}, u32[]{:S(2)}) collective-permute-start(bf16[832,512]{1,0:T(8,128)(2,1)} %param.17), channel_id=1, source_target_pairs={{0,15},{1,0},{2,1},{3,2},{4,3},{5,4},{6,5},{7,6},{8,7},{9,8},{10,9... | collective-permute-start | bytes 2555912 | tf_op jit(solution)/shard_map/ppermute | solution.py:15
  0.8 120.4 %collective-permute-start.4 = (bf16[832,512]{1,0:T(8,128)(2,1)}, bf16[832,512]{1,0:T(8,128)(2,1)}, u32[]{:S(2)}, u32[]{:S(2)}) collective-permute-start(bf16[832,512]{1,0:T(8,128)(2,1)} %param.17), channel_id=1, source_target_pairs={{0,1},{1,2},{2,3},{3,4},{4,5},{5,6},{6,7},{7,8},{8,9},{9,10},{10,1... | collective-permute-start | bytes 2555912 | tf_op jit(solution)/shard_map/ppermute | solution.py:15
  3.4 19.8 %collective-permute-start.1 = (f32[64,3]{0,1:T(4,128)}, f32[64,3]{0,1:T(4,128)S(1)}, u32[]{:S(2)}, u32[]{:S(2)}) collective-permute-start(f32[64,3]{0,1:T(4,128)} %param.14), channel_id=1, source_target_pairs={{0,15},{1,0},{2,1},{3,2},{4,3},{5,4},{6,5},{7,6},{8,7},{9,8},{10,9... | collective-permute-start | bytes 2312 | tf_op jit(solution)/shard_map/ppermute | solution.py:15
  7.2 19.2 %collective-permute-start = (bf16[64,128]{1,0:T(8,128)(2,1)S(1)}, bf16[64,128]{1,0:T(8,128)(2,1)S(1)}, u32[]{:S(2)}, u32[]{:S(2)}) collective-permute-start(bf16[64,128]{1,0:T(8,128)(2,1)S(1)} %fusion.7), channel_id=1, source_target_pairs={{0,15},{1,0},{2,1},{3,2},{4,3},{5,4},{6,5},{7,6},{8,7},{9,8},{10,9... | collective-permute-start | bytes 49160 | tf_op jit(solution)/shard_map/ppermute | solution.py:15
  13.3 13.2 %copy-start.5 = (bf16[128,256]{1,0:T(8,128)(2,1)S(1)}, bf16[128,256]{1,0:T(8,128)(2,1)}, u32[]{:S(2)}) copy-start(bf16[128,256]{1,0:T(8,128)(2,1)} %param.21) | copy-start | bytes 196612
  13.3 13.2 %copy-start.6 = (s32[2048]{0:T(1024)S(1)}, s32[2048]{0:T(1024)}, u32[]{:S(2)}) copy-start(s32[2048]{0:T(1024)} %param.15) | copy-start | bytes 24580
  26.6 2.1 %copy-start.7 = (bf16[32,256]{1,0:T(8,128)(2,1)S(1)}, bf16[32,256]{1,0:T(8,128)(2,1)}, u32[]{:S(2)}) copy-start(bf16[32,256]{1,0:T(8,128)(2,1)} %param.22) | copy-start | bytes 49156
  41.2 2.4 %copy-start.2 = (f32[64,128,169]{1,0,2:T(8,128)}, f32[64,128,169]{1,0,2:T(8,128)S(1)}, u32[]{:S(2)}) copy-start(f32[64,128,169]{1,0,2:T(8,128)S(1)} %copy.26) | copy-start | bytes 16613380
  55.1 19.7 %copy-start.8 = (f32[2,13]{1,0:T(2,128)S(1)}, f32[2,13]{1,0:T(2,128)}, u32[]{:S(2)}) copy-start(f32[2,13]{1,0:T(2,128)} %param.19) | copy-start | bytes 316
  55.1 19.7 %copy-start.9 = (s32[64]{0:T(128)S(1)}, s32[64]{0:T(128)}, u32[]{:S(2)}) copy-start(s32[64]{0:T(128)} %param.13) | copy-start | bytes 772
  74.8 46.3 %collective-permute-start.3 = (bf16[832,832]{1,0:T(8,128)(2,1)}, bf16[832,832]{1,0:T(8,128)(2,1)}, u32[]{:S(2)}, u32[]{:S(2)}) collective-permute-start(bf16[832,832]{1,0:T(8,128)(2,1)} %convert_element_type.68), channel_id=1, source_target_pairs={{0,1},{1,2},{2,3},{3,4},{4,5},{5,6},{6,7},{7,8},{8,9},{9,10},{10,1... | collective-permute-start | bytes 4153352 | tf_op jit(solution)/shard_map/ppermute | solution.py:15
  98.3 19.1 %copy-start.3 = (bf16[832,512]{1,0:T(8,128)(2,1)S(1)}, bf16[832,512]{1,0:T(8,128)(2,1)}, u32[]{:S(2)}) copy-start(bf16[832,512]{1,0:T(8,128)(2,1)} %param.17) | copy-start | bytes 2555908
  124.0 23.7 %copy-start.4 = (bf16[832,512]{1,0:T(8,128)(2,1)}, bf16[832,512]{1,0:T(8,128)(2,1)S(1)}, u32[]{:S(2)}) copy-start(bf16[832,512]{1,0:T(8,128)(2,1)S(1)} %fusion.4) | copy-start | bytes 2555908
  124.0 21.3 %collective-permute-start.5 = (bf16[832,512]{1,0:T(8,128)(2,1)S(1)}, bf16[832,512]{1,0:T(8,128)(2,1)S(1)}, u32[]{:S(2)}, u32[]{:S(2)}) collective-permute-start(bf16[832,512]{1,0:T(8,128)(2,1)S(1)} %fusion.4), channel_id=1, source_target_pairs={{0,15},{1,0},{2,1},{3,2},{4,3},{5,4},{6,5},{7,6},{8,7},{9,8},{10,9... | collective-permute-start | bytes 2555912 | tf_op jit(solution)/shard_map/ppermute | solution.py:15
  124.5 23.2 %collective-permute-start.6 = (bf16[832,512]{1,0:T(8,128)(2,1)S(1)}, bf16[832,512]{1,0:T(8,128)(2,1)S(1)}, u32[]{:S(2)}, u32[]{:S(2)}) collective-permute-start(bf16[832,512]{1,0:T(8,128)(2,1)S(1)} %fusion.4), channel_id=1, source_target_pairs={{0,1},{1,2},{2,3},{3,4},{4,5},{5,6},{6,7},{7,8},{8,9},{9,10},{10,1... | collective-permute-start | bytes 2555912 | tf_op jit(solution)/shard_map/ppermute | solution.py:15
  147.7 3.9 %copy-start.1 = (bf16[256,169]{0,1:T(8,128)(2,1)S(1)}, bf16[256,169]{0,1:T(8,128)(2,1)}, u32[]{:S(2)}) copy-start(bf16[256,169]{0,1:T(8,128)(2,1)} %param.23) | copy-start | bytes 259588
where the time goes:
time: 152 us
  local copies, waits for them, and re-layouts  75.7 us (50%)
  matrix products  30.2 us (20%)
  waiting for transfers between devices  26.7 us (18%)
  starting transfers between devices  11.8 us (8%)
  other arithmetic  6.32 us (4%)
    convert_element_type x5, local copies, waits for them, and re-layouts, as_matrix(): tiles.transpose(0, 2, 1, 3).reshape(rows_n * ORB, cols_n * ORB)  60.9 us
    ppermute x7, waiting for transfers between devices, passed_along(): return lax.ppermute(value, axis, pairs)  26.7 us
    ppermute x7, starting transfers between devices, passed_along(): return lax.ppermute(value, axis, pairs)  11.8 us
    slice x1, local copies, waits for them, and re-layouts, on_device(): own_tiles = tiles[:, :count]  6.86 us
    dot_general x2, matrix products, apply(): lax.dot_general(lower_blocks, sides[1], contract_rows, preferred_element_...  6.74 us
    convert_element_type x1, other arithmetic, as_matrix(): tiles.transpose(0, 2, 1, 3).reshape(rows_n * ORB, cols_n * ORB)  5.61 us
    dot_general x1, matrix products, place_tiles(): lax.dot_general(select, blocks, (((1,), (1,)), ((0,), (0,))), precision=l...  5.22 us
    dot_general x2, matrix products, apply(): jnp.dot(upper, sides[0], preferred_element_type=jnp.float32)  5.06 us
  transfers between devices with their start and end apart: 7, of which 2 were waited for; matrix products, arithmetic and copies ran while one was open for 68% of the time, Pallas kernels for 0%

commit v1 on v0

v1 whole, which is shorter than its diff:
```python
import functools

import jax
import jax.numpy as jnp
from jax import lax
from jax.experimental import pallas as pl
from jax.experimental.pallas import tpu as pltpu
from jax.sharding import PartitionSpec as P

ORB = 13
NRBF = 32
SPECIES = 2
NEIGH = 32
MESH = pl.DeviceIdType.MESH
F32, BF16 = jnp.float32, jnp.bfloat16
CHUNK = 512
GROUP = 8
COLS_STEP = 256


def dot(a, b):
    return jnp.dot(a, b, preferred_element_type=F32)


def dot_tn(a, b):
    return lax.dot_general(a, b, (((0,), (0,)), ((), ())), preferred_element_type=F32)


def dot_nt(a, b):
    return lax.dot_general(a, b, (((1,), (1,)), ((), ())), preferred_element_type=F32)


def split_two(v):
    high = v.astype(BF16)
    return [high, (v - high.astype(F32)).astype(BF16)]


def split_three(v):
    high = v.astype(BF16).astype(F32)
    rest = v - high
    middle = rest.astype(BF16).astype(F32)
    return jnp.concatenate([high, middle, rest - middle, jnp.zeros_like(v)], 0).astype(BF16)


def pair_tiles(own_code_at, pos_first, pos_window, terms, w_out, scale, width, tiles):
    count = tiles.shape[1]
    per_chunk = CHUNK // NEIGH
    lanes = lax.broadcasted_iota(jnp.int32, (1, CHUNK), 1) // NEIGH
    atom = lax.broadcasted_iota(jnp.int32, (count, CHUNK), 0)
    second = lax.broadcasted_iota(jnp.int32, (128, CHUNK), 0)
    centres = lax.broadcasted_iota(jnp.int32, (NRBF, 1), 0).astype(F32) * (2.0 / (NRBF - 1))
    diagonal = (
        lax.broadcasted_iota(jnp.int32, (GROUP, GROUP * NEIGH), 1) // NEIGH
        == lax.broadcasted_iota(jnp.int32, (GROUP, GROUP * NEIGH), 0)
    ).astype(F32)
    pairs = tiles.shape[0]

    @pl.loop(0, count // per_chunk)
    def _(at):
        code = own_code_at(at)
        pick_first = (atom == lanes + at * per_chunk).astype(F32).astype(BF16)
        pick_all = (second == code).astype(F32).astype(BF16)
        pick_second = pick_all[:width]
        parts = dot(pos_first, pick_first) - dot(pos_window, pick_second)
        diff = parts[0:8] + parts[8:16] + parts[16:24]
        dist_sq = jnp.sum(diff * diff, axis=0, keepdims=True)
        radial = jnp.exp(-(((dist_sq / 64.0 - centres) * 8.0) ** 2)).astype(BF16)
        picks = jnp.concatenate([pick_first, pick_first, pick_second, pick_second, radial], 0)
        pre = dot(terms, picks)
        half = pre * 0.5
        hidden = (half + half * jnp.tanh(half)).astype(BF16)
        blocks = dot(w_out, hidden) * scale
        for group in range(per_chunk // GROUP):
            span = slice(group * GROUP * NEIGH, (group + 1) * GROUP * NEIGH)
            spread = (blocks[:, None, span] * diagonal[None]).reshape(pairs * GROUP, GROUP * NEIGH)
            placed = dot_nt(spread.astype(BF16), pick_all[:, span])
            start = pl.multiple_of((at * (per_chunk // GROUP) + group) * GROUP, GROUP)
            tiles[:, pl.ds(start, GROUP), :] = placed.reshape(pairs, GROUP, 128)


def kernel(
    node_feat,
    species,
    positions,
    pair_second,
    pair_mask,
    x_vec,
    species_table,
    onsite_table,
    w_first,
    w_second,
    w_radial,
    w_out,
    first_out,
    filtered_out,
    feats,
    poss,
    codes,
    rows,
    xx,
    yy,
    tiles_own,
    tiles_prev,
    right_mat,
    left_mat,
    small_send,
    small_recv,
    x_send,
    x_recv,
    y_send,
    y_recv,
):
    n = lax.axis_size("atoms")
    me = lax.axis_index("atoms")
    right, left = lax.rem(me + 1, n), lax.rem(me + n - 1, n)
    count = node_feat.shape[0]
    cols = x_vec.shape[1]
    lane_blocks = cols // 128

    barrier = pltpu.get_barrier_semaphore()
    for neighbour in (left, right):
        pl.semaphore_signal(barrier, inc=1, device_id={"atoms": neighbour}, device_id_type=MESH)

    def send(src, dst, send_sem, recv_sem, to):
        copy = pltpu.make_async_remote_copy(
            src_ref=src,
            dst_ref=dst,
            send_sem=send_sem,
            recv_sem=recv_sem,
            device_id={"atoms": to},
            device_id_type=MESH,
        )
        copy.start()
        return copy

    spec = species[...]
    onehot = (lax.broadcasted_iota(jnp.int32, (SPECIES, count), 0) == spec).astype(F32)
    feat = (
        node_feat[...].astype(F32) + dot_tn(onehot.astype(BF16), species_table[...])
    ).astype(BF16)
    feats[1] = feat
    poss[1] = jnp.zeros(poss.shape[1:], F32)
    poss[1, 0:3, 0:count] = positions[...]
    codes[1] = jnp.where(pair_mask[...] != 0, pair_second[...], 255)
    pl.semaphore_wait(barrier, 2)

    small = [
        send(feats.at[1], feats.at[0], small_send.at[0], small_recv.at[0], right),
        send(feats.at[1], feats.at[2], small_send.at[1], small_recv.at[1], left),
        send(poss.at[1], poss.at[0], small_send.at[2], small_recv.at[2], right),
        send(poss.at[1], poss.at[2], small_send.at[3], small_recv.at[3], left),
        send(codes.at[1], codes.at[0], small_send.at[4], small_recv.at[4], right),
    ]

    for k in range(lane_blocks):
        rows[k] = x_vec[:, k * 128 : (k + 1) * 128].astype(F32)
    for k in range(lane_blocks):
        for i in range(ORB):
            xx[i, count : 2 * count, k * 128 : (k + 1) * 128] = rows[
                k, pl.ds(i, count, stride=ORB), :
            ].astype(BF16)
    x_copies = [
        send(
            xx.at[:, count : 2 * count, :],
            xx.at[:, 0:count, :],
            x_send.at[0],
            x_recv.at[0],
            right,
        ),
        send(
            xx.at[:, count : 2 * count, :],
            xx.at[:, 2 * count : 3 * count, :],
            x_send.at[1],
            x_recv.at[1],
            left,
        ),
    ]

    scale = 1.0 / jnp.sqrt(jnp.float32(2 * ORB * NEIGH))
    second_own = dot(feat, w_second[...])
    pos_own = split_three(poss[1][:, 0:count])
    onsite = lax.dot_general(
        onehot,
        onsite_table[...],
        (((0,), (0,)), ((), ())),
        precision=lax.Precision.HIGHEST,
        preferred_element_type=F32,
    )

    small[1].wait_recv()
    small[3].wait_recv()
    window = jnp.concatenate([second_own, dot(feats[2], w_second[...])], 0)
    terms = jnp.concatenate(
        split_two(dot(feat, w_first[...])) + split_two(window) + [w_radial[...]], 0
    )
    pos_window = jnp.concatenate([pos_own, split_three(poss[2][:, 0:count])], 1)

    def code_own(at):
        return codes[1, :, pl.ds(pl.multiple_of(at * CHUNK, CHUNK), CHUNK)]

    pair_tiles(
        code_own, pos_own, pos_window, terms.astype(F32).T.astype(BF16), w_out[...], scale,
        2 * count, tiles_own,
    )

    for k in (0, 2, 4):
        small[k].wait_recv()

    def code_prev(at):
        code = codes[0, :, pl.ds(pl.multiple_of(at * CHUNK, CHUNK), CHUNK)]
        return jnp.where(code < count, 255, code - count)

    terms = jnp.concatenate(
        split_two(dot(feats[0], w_first[...])) + split_two(second_own) + [w_radial[...]], 0
    )
    pair_tiles(
        code_prev, split_three(poss[0][:, 0:count]), pos_own,
        terms.astype(F32).T.astype(BF16), w_out[...], scale, count, tiles_prev,
    )

    @pl.loop(0, ORB)
    def _(i):
        for j in range(ORB):
            own = tiles_own[i * ORB + j]
            right_mat[pl.ds(pl.multiple_of(i * count, count), count), j * 128 : (j + 1) * 128] = (
                own.astype(BF16)
            )
            both = jnp.concatenate([tiles_prev[i * ORB + j], own], 0)
            left_mat[
                j * count : (j + 1) * count, pl.ds(pl.multiple_of(i * 128, 128), 128)
            ] = both.T[0:count].astype(BF16)

    def apply(vec, at):
        span = slice(at * COLS_STEP, (at + 1) * COLS_STEP)
        after = vec[:, count : 3 * count, span].reshape(ORB * 2 * count, COLS_STEP)
        before = vec[:, 0 : 2 * count, span].reshape(ORB * 2 * count, COLS_STEP)
        result = dot(right_mat[...], after) + dot(left_mat[...], before)
        here = vec[:, count : 2 * count, span].astype(F32)
        return [
            result[i * count : (i + 1) * count] + onsite[:, i : i + 1] * here[i]
            for i in range(ORB)
        ]

    for copy in x_copies:
        copy.wait_recv()
    y_copies = []
    for at in range(cols // COLS_STEP):
        span = slice(at * COLS_STEP, (at + 1) * COLS_STEP)
        step = apply(xx, at)
        for i in range(ORB):
            yy[i, count : 2 * count, span] = step[i].astype(BF16)
        for side, (place, to) in enumerate(((0, right), (2, left))):
            y_copies.append(
                send(
                    yy.at[:, count : 2 * count, span],
                    yy.at[:, place * count : (place + 1) * count, span],
                    y_send.at[2 * at + side],
                    y_recv.at[2 * at + side],
                    to,
                )
            )
        for i in range(ORB):
            for k in range(COLS_STEP // 128):
                rows[at * (COLS_STEP // 128) + k, pl.ds(i, count, stride=ORB), :] = step[i][
                    :, k * 128 : (k + 1) * 128
                ]
    for k in range(lane_blocks):
        first_out[:, k * 128 : (k + 1) * 128] = rows[k].astype(BF16)

    for at in range(cols // COLS_STEP):
        span = slice(at * COLS_STEP, (at + 1) * COLS_STEP)
        y_copies[2 * at].wait_recv()
        y_copies[2 * at + 1].wait_recv()
        step = apply(yy, at)
        for i in range(ORB):
            value = 2.0 * step[i] - xx[i, count : 2 * count, span].astype(F32)
            for k in range(COLS_STEP // 128):
                rows[at * (COLS_STEP // 128) + k, pl.ds(i, count, stride=ORB), :] = value[
                    :, k * 128 : (k + 1) * 128
                ]
        for k in range(COLS_STEP // 128):
            spot = at * (COLS_STEP // 128) + k
            filtered_out[:, spot * 128 : (spot + 1) * 128] = rows[spot]

    for copy in small + x_copies + y_copies:
        copy.wait_send()


def on_device(
    node_feat,
    species,
    positions,
    pair_second,
    pair_mask,
    x_vec,
    species_table,
    onsite_table,
    w_first,
    w_second,
    w_radial,
    w_out,
):
    count = node_feat.shape[0]
    orbs, cols = x_vec.shape
    slots = pair_second.shape[0]
    steps = cols // COLS_STEP
    vmem = pl.BlockSpec(memory_space=pltpu.VMEM)
    return pl.pallas_call(
        kernel,
        out_shape=(
            jax.ShapeDtypeStruct((orbs, cols), BF16),
            jax.ShapeDtypeStruct((orbs, cols), F32),
        ),
        in_specs=[vmem] * 12,
        out_specs=(vmem, vmem),
        scratch_shapes=[
            pltpu.VMEM((3, count, node_feat.shape[1]), BF16),
            pltpu.VMEM((3, 8, 128), F32),
            pltpu.VMEM((2, 1, slots), jnp.int32),
            pltpu.VMEM((cols // 128, orbs, 128), F32),
            pltpu.VMEM((ORB, 3 * count, cols), BF16),
            pltpu.VMEM((ORB, 3 * count, cols), BF16),
            pltpu.VMEM((ORB * ORB, count, 128), F32),
            pltpu.VMEM((ORB * ORB, count, 128), F32),
            pltpu.VMEM((orbs, ORB * 128), BF16),
            pltpu.VMEM((orbs, ORB * 128), BF16),
            pltpu.SemaphoreType.DMA((5,)),
            pltpu.SemaphoreType.DMA((5,)),
            pltpu.SemaphoreType.DMA((2,)),
            pltpu.SemaphoreType.DMA((2,)),
            pltpu.SemaphoreType.DMA((2 * steps,)),
            pltpu.SemaphoreType.DMA((2 * steps,)),
        ],
        compiler_params=pltpu.CompilerParams(
            collective_id=0, has_side_effects=True, vmem_limit_bytes=56 * 2**20
        ),
        name="pair_filter",
    )(
        node_feat,
        species.reshape(1, count),
        positions.T,
        pair_second.reshape(1, slots),
        pair_mask.reshape(1, slots),
        x_vec,
        species_table,
        onsite_table,
        w_first,
        w_second,
        w_radial,
        w_out.T,
    )


def solution(mesh):
    split = P(("groups", "atoms"))
    rows = P(("groups", "atoms"), None)
    return jax.shard_map(
        on_device,
        mesh=mesh,
        in_specs=(rows, split, rows, split, split, rows) + (P(),) * 6,
        out_specs=(rows, rows),
        check_vma=False,
    )
```

time: 152 us -> 57.6 us (0.38)
  local copies, waits for them, and re-layouts: 75.7 us -> 3.43 us
  Pallas kernels: 0 us -> 53.4 us
  matrix products: 30.2 us -> 0 us
  waiting for transfers between devices: 26.7 us -> 0 us
  starting transfers between devices: 11.8 us -> 0 us
  other arithmetic: 6.32 us -> 0 us
    convert_element_type x5 -> x0, local copies, waits for them, and re-layouts: 60.9 us -> none  [as_matrix(): tiles.transpose(0, 2, 1, 3).reshape(rows_n * ORB, cols_n * ORB)]
    pallas_call x0 -> x1, Pallas kernels: none -> 53.4 us  [on_device(): pl.pallas_call(kernel, out_shape=(jax.ShapeDtypeStruct((orbs, cols), BF16...]
    dot_general x13 -> x0, matrix products: 30.2 us -> none  [the longest x2 6.74 us: apply(): lax.dot_general(lower_blocks, sides[1], contract_rows, preferred_element_...]
    ppermute x7 -> x0, waiting for transfers between devices: 26.7 us -> none  [passed_along(): return lax.ppermute(value, axis, pairs)]
    ppermute x7 -> x0, starting transfers between devices: 11.8 us -> none  [passed_along(): return lax.ppermute(value, axis, pairs)]
    slice x1 -> x0, local copies, waits for them, and re-layouts: 6.86 us -> none  [on_device(): own_tiles = tiles[:, :count]]
    convert_element_type x1 -> x0, other arithmetic: 5.61 us -> none  [as_matrix(): tiles.transpose(0, 2, 1, 3).reshape(rows_n * ORB, cols_n * ORB)]
    mul x2 -> x0, local copies, waits for them, and re-layouts: 1.94 us -> none  [the longest x1 1.81 us: pair_blocks(): jnp.dot(hidden, w_out, preferred_element_type=jnp.float32) * factor[:, None]]
  transfers between devices with their start and end apart: 7 -> 0, of which waited for: 2 -> 0; matrix products, arithmetic and copies ran while one was open for 68% -> 0% of each run, Pallas kernels for 0% -> 0%
where the time goes in v1:
time: 57.6 us; the launch traced here: 57.5 us
  Pallas kernels  53.4 us (93%)
  local copies, waits for them, and re-layouts  3.43 us (6%)
  between operations  0.65 us (1%)
    pallas_call x1, Pallas kernels, on_device(): pl.pallas_call(kernel, out_shape=(jax.ShapeDtypeStruct((orbs, cols), BF16...  53.4 us
    unnamed x4, local copies, waits for them, and re-layouts  3.43 us

profile of v1, /device:TPU:1, one launch (start us, length us, event | category | flops | bytes accessed | tf_op | source)
XLA Modules:
  0.0 57.5 jit_solution(9816751735754709557)
XLA Ops:
  0.6 53.4 %pair_filter.1 = (bf16[832,512]{1,0:T(8,128)(2,1)}, f32[832,512]{1,0:T(8,128)}) custom-call(bf16[64,128]{1,0:T(8,128)(2,1)} %node_feat.1, s32[1,64]{1,0:T(1,128)} %bitcast.9, f32[3,64]{1,0:T(4,128)} %bitcast.8, s32[1,2048]{1,0:T(1,128)} %bitcast.6, s32[1,2048]{1,0:T(1,128)} %bitcast.7, bf16[832,512]{1,0:T(8,128)(2,1)} %x_vec.1, ...), custom_call_target="tpu_custom_call" | custom-call | tf_op jit(solution)/shard_map/pair_filter/pallas_call | solution.py:308
  54.0 0.0 copy-start
  54.0 2.2 %copy.16 = bf16[832,512]{1,0:T(8,128)(2,1)} copy(bf16[832,512]{1,0:T(8,128)(2,1)} %get-tuple-element.4) | data formatting | bytes 1703936
  56.3 0.0 copy-done
  56.3 1.2 %copy.17 = f32[832,512]{1,0:T(8,128)} copy(f32[832,512]{1,0:T(8,128)S(1)} %copy-done) | data formatting | bytes 3407872
Async XLA Ops:
  54.0 2.2 %copy-start = (f32[832,512]{1,0:T(8,128)S(1)}, f32[832,512]{1,0:T(8,128)}, u32[]{:S(2)}) copy-start(f32[832,512]{1,0:T(8,128)} %get-tuple-element.5) | copy-start | bytes 5111812

commit v2 on v1

v2 whole, which is shorter than its diff:
```python
import functools

import jax
import jax.numpy as jnp
from jax import lax
from jax.experimental import pallas as pl
from jax.experimental.pallas import tpu as pltpu
from jax.sharding import PartitionSpec as P

ORB = 13
NRBF = 32
SPECIES = 2
NEIGH = 32
MESH = pl.DeviceIdType.MESH
F32, BF16 = jnp.float32, jnp.bfloat16
CHUNK = 512
GROUP = 8
COLS_STEP = 256
SEND_STEP = 128


def dot(a, b):
    return jnp.dot(a, b, preferred_element_type=F32)


def dot_tn(a, b):
    return lax.dot_general(a, b, (((0,), (0,)), ((), ())), preferred_element_type=F32)


def dot_nt(a, b):
    return lax.dot_general(a, b, (((1,), (1,)), ((), ())), preferred_element_type=F32)


def split_two(v):
    high = v.astype(BF16)
    return [high, (v - high.astype(F32)).astype(BF16)]


def split_three(v):
    high = v.astype(BF16).astype(F32)
    rest = v - high
    middle = rest.astype(BF16).astype(F32)
    return jnp.concatenate([high, middle, rest - middle, jnp.zeros_like(v)], 0).astype(BF16)


def pair_tiles(own_code_at, pos_first, pos_window, terms, w_out, scale, width, tiles):
    count = tiles.shape[1]
    per_chunk = CHUNK // NEIGH
    lanes = lax.broadcasted_iota(jnp.int32, (1, CHUNK), 1) // NEIGH
    atom = lax.broadcasted_iota(jnp.int32, (count, CHUNK), 0)
    second = lax.broadcasted_iota(jnp.int32, (128, CHUNK), 0)
    centres = lax.broadcasted_iota(jnp.int32, (NRBF, 1), 0).astype(F32) * (2.0 / (NRBF - 1))
    diagonal = (
        lax.broadcasted_iota(jnp.int32, (GROUP, GROUP * NEIGH), 1) // NEIGH
        == lax.broadcasted_iota(jnp.int32, (GROUP, GROUP * NEIGH), 0)
    ).astype(F32)
    pairs = tiles.shape[0]

    @pl.loop(0, count // per_chunk)
    def _(at):
        code = own_code_at(at)
        pick_first = (atom == lanes + at * per_chunk).astype(F32).astype(BF16)
        pick_all = (second == code).astype(F32).astype(BF16)
        pick_second = pick_all[:width]
        parts = dot(pos_first, pick_first) - dot(pos_window, pick_second)
        diff = (parts[0:8] + parts[8:16] + parts[16:24])[0:3]
        dist_sq = jnp.sum(diff * diff, axis=0, keepdims=True)
        radial = jnp.exp(-(((dist_sq / 64.0 - centres) * 8.0) ** 2)).astype(BF16)
        picks = jnp.concatenate([pick_first, pick_first, pick_second, pick_second, radial], 0)
        pre = dot(terms, picks)
        half = pre * 0.5
        hidden = (half + half * jnp.tanh(half)).astype(BF16)
        blocks = dot(w_out, hidden) * scale
        for group in range(per_chunk // GROUP):
            span = slice(group * GROUP * NEIGH, (group + 1) * GROUP * NEIGH)
            spread = (blocks[:, None, span] * diagonal[None]).reshape(pairs * GROUP, GROUP * NEIGH)
            placed = dot_nt(spread.astype(BF16), pick_all[:, span])
            start = pl.multiple_of((at * (per_chunk // GROUP) + group) * GROUP, GROUP)
            tiles[:, pl.ds(start, GROUP), :] = placed.reshape(pairs, GROUP, 128)


def kernel(
    node_feat,
    species,
    positions,
    pair_second,
    pair_mask,
    x_vec,
    species_table,
    onsite_table,
    w_first,
    w_second,
    w_radial,
    w_out,
    first_out,
    filtered_out,
    feats,
    poss,
    codes,
    rows,
    xx,
    yy,
    tiles,
    right_mat,
    left_mat,
    small_send,
    small_recv,
    peer_send,
    cross_send,
    pass_send,
    x_recv,
    y_send,
    y_recv,
):
    n = lax.axis_size("atoms")
    me = lax.axis_index("atoms")
    spot = lax.rem(me, 4)
    odd = lax.rem(me, 2)
    own = 2 - odd
    peer = me + 1 - 2 * odd
    peer_place = 3 * odd
    upper_half = spot // 2
    cross_to = me - spot + 2 - upper_half
    middle = (spot == 1) | (spot == 2)
    pass_to = lax.rem(jnp.where(spot == 1, me + 3, me + n - 3), n)
    pass_from = 2 - 2 * upper_half
    pass_place = 2 * upper_half
    count = node_feat.shape[0]
    cols = x_vec.shape[1]
    lane_blocks = cols // 128
    pieces = cols // SEND_STEP

    def at_distance(d):
        return lax.rem(me + n + d, n)

    near = (-2, -1, 1, 2)
    barrier = pltpu.get_barrier_semaphore()
    for d in (-3, -2, -1, 1, 2, 3):
        pl.semaphore_signal(barrier, inc=1, device_id={"atoms": at_distance(d)}, device_id_type=MESH)

    def message(src, dst, send_sem, recv_sem, to):
        return pltpu.make_async_remote_copy(
            src_ref=src,
            dst_ref=dst,
            send_sem=send_sem,
            recv_sem=recv_sem,
            device_id={"atoms": to},
            device_id_type=MESH,
        )

    spec = species[...]
    onehot = (lax.broadcasted_iota(jnp.int32, (SPECIES, count), 0) == spec).astype(F32)
    feats[2] = (
        node_feat[...].astype(F32) + dot_tn(onehot.astype(BF16), species_table[...])
    ).astype(BF16)
    poss[2] = jnp.zeros(poss.shape[1:], F32)
    poss[2, 0:3, 0:count] = positions[...]
    poss[2, 3:4, 0:count] = spec.astype(F32)
    codes[2] = jnp.where(pair_mask[...] != 0, pair_second[...], 255)
    pl.semaphore_wait(barrier, 6)

    small = []
    for which, d in enumerate(near):
        for kind, array in enumerate((feats, poss, codes)):
            small.append(
                message(
                    array.at[2],
                    array.at[2 - d],
                    small_send.at[3 * which + kind],
                    small_recv.at[3 * which + kind],
                    at_distance(d),
                )
            )
    for copy in small:
        copy.start()

    def place(where):
        return pl.ds(pl.multiple_of(where * count, count), count)

    def x_message(from_place, to_place, piece, send_sem, to):
        span = slice(piece * SEND_STEP, (piece + 1) * SEND_STEP)
        return message(
            xx.at[:, place(from_place), span],
            xx.at[:, place(to_place), span],
            send_sem,
            x_recv.at[to_place, piece],
            to,
        )

    def cross_message(piece):
        return x_message(own, spot, piece, cross_send.at[piece], cross_to)

    def peer_message(piece):
        return x_message(own, peer_place, piece, peer_send.at[piece], peer)

    def pass_message(step, piece):
        return x_message(
            pass_from + step, pass_place + step, piece, pass_send.at[step, piece], pass_to
        )

    def arrived(where, piece):
        span = slice(piece * SEND_STEP, (piece + 1) * SEND_STEP)
        there = xx.at[:, place(where), span]
        message(there, there, peer_send.at[piece], x_recv.at[where, piece], peer).wait_recv()

    for k in range(lane_blocks):
        rows[k] = x_vec[:, k * 128 : (k + 1) * 128].astype(F32)
        for i in range(ORB):
            xx[i, place(own), k * 128 : (k + 1) * 128] = rows[
                k, pl.ds(i, count, stride=ORB), :
            ].astype(BF16)
        cross_message(k).start()
    for piece in range(pieces):
        peer_message(piece).start()

    scale = 1.0 / jnp.sqrt(jnp.float32(2 * ORB * NEIGH))
    base = 2 - own
    for copy in small:
        copy.wait_recv()

    seconds = [dot(feats[base + k], w_second[...]) for k in range(4)]
    sites = [split_three(poss[base + k][:, 0:count]) for k in range(4)]

    def network(k):
        window = jnp.concatenate([seconds[k], seconds[k + 1]], 0)
        terms = jnp.concatenate(
            split_two(dot(feats[base + k], w_first[...])) + split_two(window) + [w_radial[...]], 0
        )

        def code(at):
            return codes[base + k, :, pl.ds(pl.multiple_of(at * CHUNK, CHUNK), CHUNK)]

        pair_tiles(
            code, sites[k], jnp.concatenate([sites[k], sites[k + 1]], 1),
            terms.astype(F32).T.astype(BF16), w_out[...], scale, 2 * count, tiles.at[k],
        )

    def hand_on(piece):
        @pl.when(middle)
        def _():
            for step in range(2):
                arrived(pass_from + step, piece)
                pass_message(step, piece).start()

    lower_lanes = lax.broadcasted_iota(jnp.int32, (count, 2 * count), 1) < count

    def assemble(row):
        @pl.loop(0, ORB)
        def _(i):
            for j in range(ORB):
                here = tiles[row + 1, i * ORB + j]
                right_mat[row, place(i), j * 128 : (j + 1) * 128] = here.astype(BF16)
                both = jnp.concatenate([tiles[row, i * ORB + j], here], 0).T
                left_mat[
                    row, j * count : (j + 1) * count, pl.ds(pl.multiple_of(i * 128, 128), 128)
                ] = jnp.where(lower_lanes, both[count:], both[:count]).astype(BF16)

    network(0)
    hand_on(0)
    network(1)
    hand_on(1)
    assemble(0)
    network(2)
    hand_on(2)
    assemble(1)
    hand_on(3)

    def onsite_of(k):
        kind = poss[base + k][3:4, 0:count]
        pick = (lax.broadcasted_iota(jnp.int32, (SPECIES, count), 0).astype(F32) == kind).astype(F32)
        return lax.dot_general(
            pick,
            onsite_table[...],
            (((0,), (0,)), ((), ())),
            precision=lax.Precision.HIGHEST,
            preferred_element_type=F32,
        )

    def apply(vec, row, onsite, at):
        span = slice(at * COLS_STEP, (at + 1) * COLS_STEP)
        start = row * count
        if not isinstance(row, int):
            start = pl.multiple_of(start, count)
        after = vec[:, pl.ds(start + count, 2 * count), span]
        before = vec[:, pl.ds(start, 2 * count), span]
        here = after[:, 0:count].astype(F32)
        after = after.reshape(ORB * 2 * count, COLS_STEP)
        before = before.reshape(ORB * 2 * count, COLS_STEP)
        result = dot(right_mat[row], after) + dot(left_mat[row], before)
        return [
            result[i * count : (i + 1) * count] + onsite[:, i : i + 1] * here[i]
            for i in range(ORB)
        ]

    onsites = [onsite_of(1), onsite_of(2)]
    far = 2 * odd
    y_copies = []
    steps = cols // COLS_STEP
    for at in range(steps):
        span = slice(at * COLS_STEP, (at + 1) * COLS_STEP)
        for piece in range(at * COLS_STEP // SEND_STEP, (at + 1) * COLS_STEP // SEND_STEP):
            arrived(3 - 3 * odd, piece)

            @pl.when(jnp.logical_not(middle))
            def _():
                for step in range(2):
                    arrived(far + step, piece)

        for row in range(2):
            step = apply(xx, row, onsites[row], at)
            for i in range(ORB):
                yy[i, (row + 1) * count : (row + 2) * count, span] = step[i].astype(BF16)
        y_copies.append(
            message(
                yy.at[:, place(own), span],
                yy.at[:, place(peer_place), span],
                y_send.at[at],
                y_recv.at[at],
                peer,
            )
        )
        y_copies[at].start()
    for k in range(lane_blocks):
        lanes = slice(k * 128, (k + 1) * 128)
        for i in range(ORB):
            rows[k, pl.ds(i, count, stride=ORB), :] = yy[i, place(own), lanes].astype(F32)
        first_out[:, lanes] = rows[k].astype(BF16)

    onsite = jnp.where(odd == 1, onsites[0], onsites[1])
    for at in range(steps):
        span = slice(at * COLS_STEP, (at + 1) * COLS_STEP)
        y_copies[at].wait_recv()
        step = apply(yy, own - 1, onsite, at)
        for i in range(ORB):
            value = 2.0 * step[i] - xx[i, place(own), span].astype(F32)
            for k in range(COLS_STEP // 128):
                rows[at * (COLS_STEP // 128) + k, pl.ds(i, count, stride=ORB), :] = value[
                    :, k * 128 : (k + 1) * 128
                ]
        for k in range(COLS_STEP // 128):
            block = at * (COLS_STEP // 128) + k
            filtered_out[:, block * 128 : (block + 1) * 128] = rows[block]

    for copy in small + y_copies:
        copy.wait_send()
    for piece in range(pieces):
        cross_message(piece).wait_send()
        peer_message(piece).wait_send()

        @pl.when(middle)
        def _():
            for step in range(2):
                pass_message(step, piece).wait_send()


def on_device(
    node_feat,
    species,
    positions,
    pair_second,
    pair_mask,
    x_vec,
    species_table,
    onsite_table,
    w_first,
    w_second,
    w_radial,
    w_out,
):
    count = node_feat.shape[0]
    orbs, cols = x_vec.shape
    slots = pair_second.shape[0]
    steps, pieces = cols // COLS_STEP, cols // SEND_STEP
    vmem = pl.BlockSpec(memory_space=pltpu.VMEM)
    return pl.pallas_call(
        kernel,
        out_shape=(
            jax.ShapeDtypeStruct((orbs, cols), BF16),
            jax.ShapeDtypeStruct((orbs, cols), F32),
        ),
        in_specs=[vmem] * 12,
        out_specs=(vmem, vmem),
        scratch_shapes=[
            pltpu.VMEM((5, count, node_feat.shape[1]), BF16),
            pltpu.VMEM((5, 8, 128), F32),
            pltpu.VMEM((5, 1, slots), jnp.int32),
            pltpu.VMEM((cols // 128, orbs, 128), F32),
            pltpu.VMEM((ORB, 4 * count, cols), BF16),
            pltpu.VMEM((ORB, 4 * count, cols), BF16),
            pltpu.VMEM((3, ORB * ORB, count, 128), F32),
            pltpu.VMEM((2, orbs, ORB * 128), BF16),
            pltpu.VMEM((2, orbs, ORB * 128), BF16),
            pltpu.SemaphoreType.DMA((12,)),
            pltpu.SemaphoreType.DMA((12,)),
            pltpu.SemaphoreType.DMA((pieces,)),
            pltpu.SemaphoreType.DMA((pieces,)),
            pltpu.SemaphoreType.DMA((2, pieces)),
            pltpu.SemaphoreType.DMA((4, pieces)),
            pltpu.SemaphoreType.DMA((steps,)),
            pltpu.SemaphoreType.DMA((steps,)),
        ],
        compiler_params=pltpu.CompilerParams(
            collective_id=0, has_side_effects=True, vmem_limit_bytes=58 * 2**20
        ),
        name="pair_filter",
    )(
        node_feat,
        species.reshape(1, count),
        positions.T,
        pair_second.reshape(1, slots),
        pair_mask.reshape(1, slots),
        x_vec,
        species_table,
        onsite_table,
        w_first,
        w_second,
        w_radial,
        w_out.T,
    )


def solution(mesh):
    split = P(("groups", "atoms"))
    rows = P(("groups", "atoms"), None)
    return jax.shard_map(
        on_device,
        mesh=mesh,
        in_specs=(rows, split, rows, split, split, rows) + (P(),) * 6,
        out_specs=(rows, rows),
        check_vma=False,
    )
```

time: 57.6 us -> 55.4 us (0.962)
  the two profiles are of different devices: /device:TPU:1 before, /device:TPU:0 now
where the time goes in v2:
time: 55.4 us; the launch traced here: 55.3 us
  Pallas kernels  51.2 us (92%)
  local copies, waits for them, and re-layouts  3.43 us (6%)
  between operations  0.65 us (1%)
    pallas_call x1, Pallas kernels, on_device(): pl.pallas_call(kernel, out_shape=(jax.ShapeDtypeStruct((orbs, cols), BF16...  51.2 us
    unnamed x4, local copies, waits for them, and re-layouts  3.43 us

profile of v2, /device:TPU:0, one launch (start us, length us, event | category | flops | bytes accessed | tf_op | source)
XLA Modules:
  0.0 55.3 jit_solution(5430344416991328426)
XLA Ops:
  0.6 51.2 %pair_filter.1 = (bf16[832,512]{1,0:T(8,128)(2,1)}, f32[832,512]{1,0:T(8,128)}) custom-call(bf16[64,128]{1,0:T(8,128)(2,1)} %node_feat.1, s32[1,64]{1,0:T(1,128)} %bitcast.9, f32[3,64]{1,0:T(4,128)} %bitcast.8, s32[1,2048]{1,0:T(1,128)} %bitcast.6, s32[1,2048]{1,0:T(1,128)} %bitcast.7, bf16[832,512]{1,0:T(8,128)(2,1)} %x_vec.1, ...), custom_call_target="tpu_custom_call" | custom-call | tf_op jit(solution)/shard_map/pair_filter/pallas_call | solution.py:375
  51.8 0.0 copy-start
  51.9 2.2 %copy.16 = bf16[832,512]{1,0:T(8,128)(2,1)} copy(bf16[832,512]{1,0:T(8,128)(2,1)} %get-tuple-element.4) | data formatting | bytes 1703936
  54.1 0.0 copy-done
  54.1 1.2 %copy.17 = f32[832,512]{1,0:T(8,128)} copy(f32[832,512]{1,0:T(8,128)S(1)} %copy-done) | data formatting | bytes 3407872
Async XLA Ops:
  51.8 2.2 %copy-start = (f32[832,512]{1,0:T(8,128)S(1)}, f32[832,512]{1,0:T(8,128)}, u32[]{:S(2)}) copy-start(f32[832,512]{1,0:T(8,128)} %get-tuple-element.5) | copy-start | bytes 5111812

commit v3 on v2

--- a/solution.py
+++ b/solution.py
@@ -157,6 +157,16 @@
     poss[2, 0:3, 0:count] = positions[...]
     poss[2, 3:4, 0:count] = spec.astype(F32)
     codes[2] = jnp.where(pair_mask[...] != 0, pair_second[...], 255)
+
+    def place(where):
+        return pl.ds(pl.multiple_of(where * count, count), count)
+
+    for k in range(lane_blocks):
+        rows[k] = x_vec[:, k * 128 : (k + 1) * 128].astype(F32)
+        for i in range(ORB):
+            xx[i, place(own), k * 128 : (k + 1) * 128] = rows[
+                k, pl.ds(i, count, stride=ORB), :
+            ].astype(BF16)
     pl.semaphore_wait(barrier, 6)
 
     small = []
@@ -174,9 +184,6 @@
     for copy in small:
         copy.start()
 
-    def place(where):
-        return pl.ds(pl.multiple_of(where * count, count), count)
-
     def x_message(from_place, to_place, piece, send_sem, to):
         span = slice(piece * SEND_STEP, (piece + 1) * SEND_STEP)
         return message(
@@ -203,13 +210,8 @@
         there = xx.at[:, place(where), span]
         message(there, there, peer_send.at[piece], x_recv.at[where, piece], peer).wait_recv()
 
-    for k in range(lane_blocks):
-        rows[k] = x_vec[:, k * 128 : (k + 1) * 128].astype(F32)
-        for i in range(ORB):
-            xx[i, place(own), k * 128 : (k + 1) * 128] = rows[
-                k, pl.ds(i, count, stride=ORB), :
-            ].astype(BF16)
-        cross_message(k).start()
+    for piece in range(pieces):
+        cross_message(piece).start()
     for piece in range(pieces):
         peer_message(piece).start()
 
@@ -375,8 +377,8 @@
     return pl.pallas_call(
         kernel,
         out_shape=(
-            jax.ShapeDtypeStruct((orbs, cols), BF16),
-            jax.ShapeDtypeStruct((orbs, cols), F32),
+            pltpu.VMEM((orbs, cols), BF16),
+            pltpu.VMEM((orbs, cols), F32),
         ),
         in_specs=[vmem] * 12,
         out_specs=(vmem, vmem),

time: 55.4 us -> 52.6 us (0.949)
  Pallas kernels: 51.2 us -> 49.8 us
  local copies, waits for them, and re-layouts: 3.43 us -> 2.09 us
    pallas_call x1, Pallas kernels: 51.2 us -> 49.8 us  [on_device(): pl.pallas_call(kernel, out_shape=(pltpu.VMEM((orbs, cols), BF16), pltpu.V...]
    unnamed x4 -> x2, local copies, waits for them, and re-layouts: 3.43 us -> 2.09 us
where the time goes in v3:
time: 52.6 us; the launch traced here: 52.5 us
  Pallas kernels  49.8 us (95%)
  local copies, waits for them, and re-layouts  2.09 us (4%)
  between operations  0.64 us (1%)
    pallas_call x1, Pallas kernels, on_device(): pl.pallas_call(kernel, out_shape=(pltpu.VMEM((orbs, cols), BF16), pltpu.V...  49.8 us
    unnamed x2, local copies, waits for them, and re-layouts  2.09 us

profile of v3, /device:TPU:0, one launch (start us, length us, event | category | flops | bytes accessed | tf_op | source)
XLA Modules:
  0.0 52.5 jit_solution(7611023049330381374)
XLA Ops:
  0.6 49.8 %pair_filter.1 = (bf16[832,512]{1,0:T(8,128)(2,1)S(1)}, f32[832,512]{1,0:T(8,128)S(1)}) custom-call(bf16[64,128]{1,0:T(8,128)(2,1)} %node_feat.1, s32[1,64]{1,0:T(1,128)} %bitcast.9, f32[3,64]{1,0:T(4,128)} %bitcast.8, s32[1,2048]{1,0:T(1,128)} %bitcast.6, s32[1,2048]{1,0:T(1,128)} %bitcast.7, bf16[832,512]{1,0:T(8,128)(2,1)} %x_vec.1, ...), custom_call_target="tpu_custom_call" | custom-call | tf_op jit(solution)/shard_map/pair_filter/pallas_call | solution.py:377
  50.4 0.9 %copy.16 = bf16[832,512]{1,0:T(8,128)(2,1)} copy(bf16[832,512]{1,0:T(8,128)(2,1)S(1)} %get-tuple-element.2) | data formatting | bytes 1703936
  51.3 1.2 %copy.17 = f32[832,512]{1,0:T(8,128)} copy(f32[832,512]{1,0:T(8,128)S(1)} %get-tuple-element.3) | data formatting | bytes 3407872
